TPU v7x, 32 devices: a whole 2x2x4 slice. The times are simulated.
32 devices in a mesh: groups: 2 (over y), pair: 8 (over z, x), aux: 2 (over core).
Axes of the slice: x: 2, y: 2, z: 4, core: 2. Of those that a mesh axis runs over, the one named last changes fastest.
Arguments:
- factors: float32 [8192, 2048], P(('groups', 'pair', 'aux')), parts along dimension 0, may hold values from -0.6 to 0.6
- occupied_energy: float32 [256], P('groups'), parts along dimension 0, may hold values from -3 to -0.4
- virtual_energy: float32 [4096], P('groups'), parts along dimension 0, may hold values from 0.2 to 4
- batch_orbitals: int32 [2], P('groups'), parts along dimension 0, may hold values from 0 to 127, as said below
- panel_order: int32 [32], P('groups'), parts along dimension 0, may hold values from 0 to 31, as said below
Outputs:
- density: float32 [8192, 2048], P(('groups', 'pair', 'aux')), parts along dimension 0
There are 2 independent parts, one for each index of `groups`. A program takes and returns all parts, laid end to end along the dimension named above; each array names one. Nothing has to cross between parts.
Inputs may be any that keep to these rules, and one draw needn't show every extreme that they name: `batch_orbitals`: 1 distinct occupied orbitals. `panel_order`: 16 distinct panel numbers.
All inputs are finite; a program needn't handle non-finite values.
Results may differ from a plain program's by a relative error of at most 0.0001.
Values sent between devices are 32-bit elements; how exact they have to be, the bound alone decides.
A program may use at most 64 MiB of HBM per device.

v0:
```python
import jax
import jax.numpy as jnp
from jax import lax
from jax.sharding import PartitionSpec as P

PANEL = 64
os_scale = 1.3


def spread(block, axis, source):
    block = jnp.where(lax.axis_index(axis) == source, block, jnp.zeros_like(block))
    return lax.psum(block, axis)


def column_energies(columns, batch_energy, virtual_energy):
    nvir = virtual_energy.shape[0]
    nbatch = batch_energy.shape[0]
    orbital = columns // nvir
    virtual = columns % nvir
    occ_part = jnp.sum(
        jnp.where(
            orbital[:, None] == jnp.arange(nbatch, dtype=jnp.int32)[None, :],
            batch_energy[None, :],
            0.0,
        ),
        axis=1,
    )
    vir_part = jnp.sum(
        jnp.where(
            virtual[:, None] == jnp.arange(nvir, dtype=jnp.int32)[None, :],
            virtual_energy[None, :],
            0.0,
        ),
        axis=1,
    )
    return vir_part - occ_part


def batch_energies(occupied_energy, batch_orbitals):
    noccupied = occupied_energy.shape[0]
    return jnp.sum(
        jnp.where(
            batch_orbitals[:, None] == jnp.arange(noccupied, dtype=jnp.int32)[None, :],
            occupied_energy[None, :],
            0.0,
        ),
        axis=1,
    )


def by_columns(factors, occupied_energy, virtual_energy, batch_orbitals, panel_order):
    pair_count = lax.axis_size("pair")
    total_columns = factors.shape[1]
    col_local = total_columns // pair_count
    per_owner = col_local // PANEL
    working = lax.all_to_all(factors, "pair", split_axis=1, concat_axis=0, tiled=True)
    batch_energy = batch_energies(occupied_energy, batch_orbitals)
    own_columns = lax.axis_index("pair") * col_local + jnp.arange(col_local, dtype=jnp.int32)
    own_energy = column_energies(own_columns, batch_energy, virtual_energy)

    def one_panel(position, density):
        number = panel_order[position]
        owner_index = number // per_owner
        panel_slab = lax.dynamic_slice_in_dim(working, number % per_owner * PANEL, PANEL, 1)
        panel_block = spread(panel_slab, "pair", owner_index)
        panel_energy = column_energies(
            number * PANEL + jnp.arange(PANEL, dtype=jnp.int32), batch_energy, virtual_energy
        )
        partial_ints = lax.dot_general(
            panel_block,
            working,
            (((0,), (0,)), ((), ())),
            precision=lax.Precision.HIGHEST,
            preferred_element_type=jnp.float32,
        )
        integrals = lax.psum(partial_ints, "aux")
        amplitudes = os_scale * integrals / (own_energy[None, :] + panel_energy[:, None])
        return density + jnp.dot(
            panel_block,
            amplitudes,
            precision=lax.Precision.HIGHEST,
            preferred_element_type=jnp.float32,
        )

    density = lax.fori_loop(
        0, panel_order.shape[0], one_panel, jnp.zeros(working.shape, jnp.float32)
    )
    return lax.all_to_all(density, "pair", split_axis=0, concat_axis=1, tiled=True)


def by_rows(factors, occupied_energy, virtual_energy, batch_orbitals, panel_order):
    total = factors.shape[1]
    batch_energy = batch_energies(occupied_energy, batch_orbitals)
    nvir = virtual_energy.shape[0]
    energy = (virtual_energy[None, :] - batch_energy[:, None]).reshape(-1)
    panels = jnp.concatenate(
        [
            lax.dynamic_slice_in_dim(factors, panel_order[k] * PANEL, PANEL, 1)
            for k in range(panel_order.shape[0])
        ],
        axis=1,
    )
    chosen = jnp.concatenate(
        [
            lax.dynamic_slice_in_dim(energy, panel_order[k] * PANEL, PANEL, 0)
            for k in range(panel_order.shape[0])
        ]
    )
    partial = lax.dot_general(
        panels,
        factors,
        (((0,), (0,)), ((), ())),
        precision=lax.Precision.HIGH,
        preferred_element_type=jnp.float32,
    )
    mine = lax.psum_scatter(partial, ("pair", "aux"), scatter_dimension=0, tiled=True)
    rank = lax.axis_index("pair") * lax.axis_size("aux") + lax.axis_index("aux")
    my_energy = lax.dynamic_slice_in_dim(chosen, rank * mine.shape[0], mine.shape[0], 0)
    mine = os_scale * mine / (energy[None, :] + my_energy[:, None])
    amplitudes = lax.all_gather(mine, ("pair", "aux"), axis=0, tiled=True)
    return jnp.dot(
        panels, amplitudes, precision=lax.Precision.HIGH, preferred_element_type=jnp.float32
    )


def on_device(factors, occupied_energy, virtual_energy, batch_orbitals, panel_order):
    window = panel_order.shape[0] * PANEL
    fits = 4 * window * factors.shape[1] <= 8 * 1024 * 1024
    plan = by_rows if fits else by_columns
    return plan(factors, occupied_energy, virtual_energy, batch_orbitals, panel_order)


def solution(mesh):
    in_specs = (
        P(("groups", "pair", "aux"), None),
        P("groups"),
        P("groups"),
        P("groups"),
        P("groups"),
    )
    out_specs = P(("groups", "pair", "aux"), None)
    return jax.shard_map(
        on_device, mesh=mesh, in_specs=in_specs, out_specs=out_specs, check_vma=False
    )
```

profile of v0, /device:TPU:0, one launch (start us, length us, event | category | flops | bytes accessed | tf_op | source)
XLA Modules:
  0.0 228.8 jit_solution(1374346407316018232)
XLA Ops:
  6.5 0.0 reduce-scatter.2.cloned.1.call-start
  6.5 2.0 fusion.2
  18.7 3.4 %constant_dynamic-slice_fusion = (f32[256,64]{1,0:T(8,128)S(1)}, f32[256,64]{1,0:T(8,128)S(1)}, f32[256,64]{1,0:T(8,128)S(1)}, f32[256,64]{1,0:T(8,128)}, f32[25...) fusion(f32[256,2048]{1,0:T(8,128)} %param.5, ...), kind=kLoop, calls=%fused_computation.2 | loop fusion | bytes 2097216 | tf_op jit(solution)/shard_map/dynamic_slice | solution.py:98
  22.1 0.0 copy-start
  22.1 1.9 concatenate.6
  24.0 0.3 copy-done
  24.3 5.8 %fusion.3 = f32[1024,2048]{1,0:T(8,128)} fusion(f32[256,1024]{1,0:T(8,128)S(1)} %concatenate.6, f32[256,2048]{1,0:T(8,128)S(1)} %copy-done), kind=kOutput, calls=%fused_computation.22 | convolution fusion | flops 3221225472 | bytes 11534336 | tf_op jit(solution)/shard_map/dot_general | solution.py:109
  30.1 0.0 copy-start.2
  30.1 0.0 copy-start.1
  30.1 0.0 reduce-scatter.2.cloned.1.call-update
  30.1 0.0 all-gather.2.cloned.1.call-start
  30.8 0.0 copy-done.2
  30.8 0.6 fusion
  31.5 0.0 copy-done.1
  31.5 0.6 broadcast_subtract_fusion
  32.1 0.2 fusion.1
  32.3 0.1 concatenate.7
  32.3 0.1 dynamic_slice.131
  32.4 105.1 %reduce-scatter.2.cloned.1.call-done = f32[64,2048]{1,0:T(8,128)} async-done(((f32[1024,2048]{1,0:T(8,128)}), f32[64,2048]{1,0:T(8,128)}) %reduce-scatter.2.cloned.1.call-update) | async-done | bytes 524304 | tf_op jit(solution)/shard_map/reduce_scatter | solution.py:116
  137.6 2.0 add_divide_fusion
  139.6 0.0 all-gather.2.cloned.1.call-update
  139.6 74.8 %all-gather.2.cloned.1.call-done = f32[1024,2048]{1,0:T(8,128)} async-done(((f32[64,2048]{1,0:T(8,128)}), f32[1024,2048]{1,0:T(8,128)}) %all-gather.2.cloned.1.call-update) | async-done | bytes 8388624 | tf_op jit(solution)/shard_map/all_gather | solution.py:120
  214.4 7.6 %fusion.4 = f32[256,2048]{1,0:T(8,128)} fusion(f32[256,1024]{1,0:T(8,128)S(1)} %concatenate.6, f32[1024,2048]{1,0:T(8,128)} %all-gather.2.cloned.1.call-done), kind=kOutput, calls=%fused_computation.23 | convolution fusion | flops 3221225472 | bytes 11534336 | tf_op jit(solution)/shard_map/dot_general | solution.py:121
Async XLA Ops:
  6.5 131.0 %reduce-scatter.2.cloned.1.call-start = ((), (), s32[]{:S(2)}) async-start(), calls=%async_computation.1 | async-start | bytes 8912896 | tf_op jit(solution)/shard_map/reduce_scatter | solution.py:116
  22.1 2.2 copy-start
  30.1 0.7 copy-start.2
  30.1 1.4 copy-start.1
  30.1 184.3 %all-gather.2.cloned.1.call-start = ((), (), s32[]{:S(2)}) async-start(), calls=%async_computation.2 | async-start | bytes 8912896 | tf_op jit(solution)/shard_map/all_gather | solution.py:120
Sparse Core Ops, SparseCore 0:
  30.2 107.2 reduce-scatter.1
  139.7 74.6 all-gather.1
where the time goes:
time: 229 us
  waiting for transfers between devices  180 us (79%)
  between operations  24.3 us (11%)
  matrix products  13.4 us (6%)
  local copies, waits for them, and re-layouts  7.91 us (3%)
  other arithmetic  3.25 us (1%)
    reduce_scatter x1, waiting for transfers between devices, by_rows(): lax.psum_scatter(partial, ('pair', 'aux'), scatter_dimension=0, tiled=True)  105 us
    all_gather x1, waiting for transfers between devices, by_rows(): amplitudes = lax.all_gather(mine, ('pair', 'aux'), axis=0, tiled=True)  74.8 us
    dot_general x1, matrix products, by_rows(): jnp.dot(panels, amplitudes, precision=lax.Precision.HIGH, preferred_eleme...  7.56 us
    dot_general x1, matrix products, by_rows(): lax.dot_general(panels, factors, (((0,), (0,)), ((), ())), precision=lax....  5.8 us
  transfers between devices with their start and end apart: 2, of which 2 were waited for; matrix products, arithmetic and copies ran while one was open for 1% of the time, Pallas kernels for 0%

commit v1 on v0

--- a/solution.py
+++ b/solution.py
@@ -5,6 +5,27 @@
 
 PANEL = 64
 os_scale = 1.3
+
+
+def gather_around(x, axis, dim):
+    size, position, extent = (lax.axis_size(axis), lax.axis_index(axis), x.shape[dim])
+    upward = [(i, (i + 1) % size) for i in range(size)]
+    left = [(i, (i - 1) % size) for i in range(size)]
+    whole = jnp.zeros((*x.shape[:dim], size * extent, *x.shape[dim + 1 :]), x.dtype)
+    whole = lax.dynamic_update_slice_in_dim(whole, x, position * extent, axis=dim)
+    from_left = from_right = x
+    middle = size // 2
+    for step in range(1, middle + 1):
+        from_left = lax.ppermute(from_left, axis, upward)
+        whole = lax.dynamic_update_slice_in_dim(
+            whole, from_left, (position - step) % size * extent, axis=dim
+        )
+        if step < size - middle:
+            from_right = lax.ppermute(from_right, axis, left)
+            whole = lax.dynamic_update_slice_in_dim(
+                whole, from_right, (position + step) % size * extent, axis=dim
+            )
+    return whole
 
 
 def spread(block, axis, source):
@@ -117,7 +138,7 @@
     rank = lax.axis_index("pair") * lax.axis_size("aux") + lax.axis_index("aux")
     my_energy = lax.dynamic_slice_in_dim(chosen, rank * mine.shape[0], mine.shape[0], 0)
     mine = os_scale * mine / (energy[None, :] + my_energy[:, None])
-    amplitudes = lax.all_gather(mine, ("pair", "aux"), axis=0, tiled=True)
+    amplitudes = gather_around(mine, ("pair", "aux"), 0)
     return jnp.dot(
         panels, amplitudes, precision=lax.Precision.HIGH, preferred_element_type=jnp.float32
     )

time: 229 us -> 264 us (1.15)
  the two profiles are of different devices: /device:TPU:0 before, /device:TPU:10 now
where the time goes in v1:
time: 264 us; the launch traced here: 263 us
  waiting for transfers between devices  182 us (69%)
  local copies, waits for them, and re-layouts  27.6 us (10%)
  between operations  24.7 us (9%)
  matrix products  13.4 us (5%)
  starting transfers between devices  13.1 us (5%)
    reduce_scatter x1, waiting for transfers between devices, by_rows(): lax.psum_scatter(partial, ('pair', 'aux'), scatter_dimension=0, tiled=True)  104 us
    ppermute x8, waiting for transfers between devices, gather_around(): from_left = lax.ppermute(from_left, axis, upward)  49.8 us
    ppermute x7, waiting for transfers between devices, gather_around(): from_right = lax.ppermute(from_right, axis, left)  28.6 us
    ppermute x7, starting transfers between devices, gather_around(): from_right = lax.ppermute(from_right, axis, left)  13 us
    dynamic_update_slice x7, local copies, waits for them, and re-layouts, gather_around(): lax.dynamic_update_slice_in_dim(whole, from_right, (position + step) % si...  7.94 us
    dynamic_update_slice x8, local copies, waits for them, and re-layouts, gather_around(): lax.dynamic_update_slice_in_dim(whole, from_left, (position - step) % siz...  7.78 us
    dot_general x1, matrix products, by_rows(): jnp.dot(panels, amplitudes, precision=lax.Precision.HIGH, preferred_eleme...  7.56 us
    dot_general x1, matrix products, by_rows(): lax.dot_general(panels, factors, (((0,), (0,)), ((), ())), precision=lax....  5.83 us
  transfers between devices with their start and end apart: 16, of which 12 were waited for; matrix products, arithmetic and copies ran while one was open for 6% of the time, Pallas kernels for 0%

profile of v1, /device:TPU:10, one launch (start us, length us, event | category | flops | bytes accessed | tf_op | source)
XLA Modules:
  0.0 263.2 jit_solution(8015272161731179169)
XLA Ops:
  6.5 1.9 fusion.2
  18.7 3.4 %constant_dynamic-slice_fusion = (f32[256,64]{1,0:T(8,128)S(1)}, f32[256,64]{1,0:T(8,128)S(1)}, f32[256,64]{1,0:T(8,128)S(1)}, f32[256,64]{1,0:T(8,128)}, f32[25...) fusion(f32[256,2048]{1,0:T(8,128)} %param.5, ...), kind=kLoop, calls=%fused_computation.17 | loop fusion | bytes 2097216 | tf_op jit(solution)/shard_map/dynamic_slice | solution.py:119
  22.2 1.8 concatenate.6
  24.0 5.8 %fusion.3 = f32[1024,2048]{1,0:T(8,128)} fusion(f32[256,1024]{1,0:T(8,128)S(1)} %concatenate.6, f32[256,2048]{1,0:T(8,128)S(1)} %copy-done), kind=kOutput, calls=%fused_computation.38 | convolution fusion | flops 3221225472 | bytes 11534336 | tf_op jit(solution)/shard_map/dot_general | solution.py:130
  32.1 103.9 %reduce-scatter.2.cloned.1.call-done = f32[64,2048]{1,0:T(8,128)} async-done(((f32[1024,2048]{1,0:T(8,128)}), f32[64,2048]{1,0:T(8,128)}) %reduce-scatter.2.cloned.1.call-update) | async-done | bytes 524304 | tf_op jit(solution)/shard_map/reduce_scatter | solution.py:137
  136.0 4.3 %broadcast_in_dim.6 = f32[1024,2048]{1,0:T(8,128)} broadcast(f32[]{:T(128)} %constant.130.clone.1), dimensions={} | broadcast | bytes 8388612 | tf_op jit(solution)/shard_map/broadcast_in_dim | solution.py:14
  140.3 1.0 constant_dynamic-update-slice_fusion.15
  141.2 1.7 collective-permute-start.1
  143.0 12.5 %collective-permute-done = f32[64,2048]{1,0:T(8,128)S(1)} collective-permute-done((f32[64,2048]{1,0:T(8,128)S(1)}, f32[64,2048]{1,0:T(8,128)S(1)}, u32[]{:S(2)}, u32[]{:S(2)}) %collective-permute-start) | collective-permute-done | bytes 524320 | tf_op jit(solution)/shard_map/ppermute | solution.py:19
  155.5 4.6 %collective-permute-done.1 = f32[64,2048]{1,0:T(8,128)S(1)} collective-permute-done((f32[64,2048]{1,0:T(8,128)S(1)}, f32[64,2048]{1,0:T(8,128)S(1)}, u32[]{:S(2)}, u32[]{:S(2)}) %collective-permute-start.1) | collective-permute-done | bytes 524320 | tf_op jit(solution)/shard_map/ppermute | solution.py:24
  160.0 1.9 collective-permute-start.3
  161.9 6.4 %collective-permute-done.2 = f32[64,2048]{1,0:T(8,128)S(1)} collective-permute-done((f32[64,2048]{1,0:T(8,128)S(1)}, f32[64,2048]{1,0:T(8,128)S(1)}, u32[]{:S(2)}, u32[]{:S(2)}) %collective-permute-start.2) | collective-permute-done | bytes 524320 | tf_op jit(solution)/shard_map/ppermute | solution.py:19
  168.4 10.9 %collective-permute-done.3 = f32[64,2048]{1,0:T(8,128)} collective-permute-done((f32[64,2048]{1,0:T(8,128)S(1)}, f32[64,2048]{1,0:T(8,128)}, u32[]{:S(2)}, u32[]{:S(2)}) %collective-permute-start.3) | collective-permute-done | bytes 524320 | tf_op jit(solution)/shard_map/ppermute | solution.py:24
  179.3 2.0 collective-permute-start.5
  181.6 1.9 constant_dynamic-update-slice_fusion.14
  183.5 10.4 %collective-permute-done.5 = f32[64,2048]{1,0:T(8,128)S(1)} collective-permute-done((f32[64,2048]{1,0:T(8,128)}, f32[64,2048]{1,0:T(8,128)S(1)}, u32[]{:S(2)}, u32[]{:S(2)}) %collective-permute-start.5) | collective-permute-done | bytes 524320 | tf_op jit(solution)/shard_map/ppermute | solution.py:24
  193.9 1.8 collective-permute-start.7
  195.7 1.9 constant_dynamic-update-slice_fusion.13
  198.4 1.9 constant_dynamic-update-slice_fusion.11
  200.3 2.1 collective-permute-done.7
  202.4 1.9 collective-permute-start.9
  204.3 0.9 constant_dynamic-update-slice_fusion.10
  205.2 6.6 %collective-permute-done.8 = f32[64,2048]{1,0:T(8,128)S(1)} collective-permute-done((f32[64,2048]{1,0:T(8,128)S(1)}, f32[64,2048]{1,0:T(8,128)S(1)}, u32[]{:S(2)}, u32[]{:S(2)}) %collective-permute-start.8) | collective-permute-done | bytes 524320 | tf_op jit(solution)/shard_map/ppermute | solution.py:19
  214.2 1.9 collective-permute-start.11
  216.9 8.2 %collective-permute-done.10 = f32[64,2048]{1,0:T(8,128)S(1)} collective-permute-done((f32[64,2048]{1,0:T(8,128)S(1)}, f32[64,2048]{1,0:T(8,128)S(1)}, u32[]{:S(2)}, u32[]{:S(2)}) %collective-permute-start.10) | collective-permute-done | bytes 524320 | tf_op jit(solution)/shard_map/ppermute | solution.py:19
  226.0 0.8 constant_dynamic-update-slice_fusion.5
  226.8 1.7 collective-permute-start.13
  228.6 0.8 constant_dynamic-update-slice_fusion.4
  229.4 9.9 %collective-permute-done.12 = f32[64,2048]{1,0:T(8,128)S(1)} collective-permute-done((f32[64,2048]{1,0:T(8,128)S(1)}, f32[64,2048]{1,0:T(8,128)S(1)}, u32[]{:S(2)}, u32[]{:S(2)}) %collective-permute-start.12) | collective-permute-done | bytes 524320 | tf_op jit(solution)/shard_map/ppermute | solution.py:19
  240.2 0.9 constant_dynamic-update-slice_fusion.2
  241.9 6.1 %collective-permute-done.14 = f32[64,2048]{1,0:T(8,128)S(1)} collective-permute-done((f32[64,2048]{1,0:T(8,128)S(1)}, f32[64,2048]{1,0:T(8,128)S(1)}, u32[]{:S(2)}, u32[]{:S(2)}) %collective-permute-start.14) | collective-permute-done | bytes 524320 | tf_op jit(solution)/shard_map/ppermute | solution.py:19
  248.8 7.6 %fusion.4 = f32[256,2048]{1,0:T(8,128)} fusion(f32[256,1024]{1,0:T(8,128)S(1)} %concatenate.6, f32[1024,2048]{1,0:T(8,128)} %constant_dynamic-update-slice_fusion), kind=kOutput, calls=%fused_computation.39 | convolution fusion | flops 3221225472 | bytes 11534336 | tf_op jit(solution)/shard_map/dot_general | solution.py:142
  (40 shorter events, 9.1 us)
Async XLA Ops:
  6.5 17.4 %copy-start = (f32[256,2048]{1,0:T(8,128)S(1)}, f32[256,2048]{1,0:T(8,128)}, u32[]{:S(2)}) copy-start(f32[256,2048]{1,0:T(8,128)} %param.5) | copy-start | bytes 6291460
  6.5 129.4 %reduce-scatter.2.cloned.1.call-start = ((), (), s32[]{:S(2)}) async-start(), calls=%async_computation.1 | async-start | bytes 8912896 | tf_op jit(solution)/shard_map/reduce_scatter | solution.py:137
  24.0 6.5 %copy-start.5 = (f32[128]{0:T(128)S(1)}, f32[128]{0:T(128)}, u32[]{:S(2)}) copy-start(f32[128]{0:T(128)} %param.6) | copy-start | bytes 1540
  24.0 7.2 %copy-start.4 = (f32[2048]{0:T(1024)S(1)}, f32[2048]{0:T(1024)}, u32[]{:S(2)}) copy-start(f32[2048]{0:T(1024)} %param.7) | copy-start | bytes 24580
  136.0 4.3 %copy-start.3 = (f32[64,2048]{1,0:T(8,128)S(1)}, f32[64,2048]{1,0:T(8,128)}, u32[]{:S(2)}) copy-start(f32[64,2048]{1,0:T(8,128)} %reduce-scatter.2.cloned.1.call-done) | copy-start | bytes 1572868
  141.2 14.2 %collective-permute-start = (f32[64,2048]{1,0:T(8,128)S(1)}, f32[64,2048]{1,0:T(8,128)S(1)}, u32[]{:S(2)}, u32[]{:S(2)}) collective-permute-start(f32[64,2048]{1,0:T(8,128)S(1)} %get-tuple-element.6), channel_id=1, source_target_pairs={{0,1},{1,2},{2,3},{3,4},{4,5},{5,6},{6,7},{7,8},{8,9},{9,10},{10,1... | collective-permute-start | bytes 1572872 | tf_op jit(solution)/shard_map/ppermute | solution.py:19
  141.2 18.8 %collective-permute-start.1 = (f32[64,2048]{1,0:T(8,128)S(1)}, f32[64,2048]{1,0:T(8,128)S(1)}, u32[]{:S(2)}, u32[]{:S(2)}) collective-permute-start(f32[64,2048]{1,0:T(8,128)S(1)} %get-tuple-element.6), channel_id=1, source_target_pairs={{0,15},{1,0},{2,1},{3,2},{4,3},{5,4},{6,5},{7,6},{8,7},{9,8},{10,9... | collective-permute-start | bytes 1572872 | tf_op jit(solution)/shard_map/ppermute | solution.py:24
  155.5 25.8 %copy-start.2 = (f32[64,2048]{1,0:T(8,128)}, f32[64,2048]{1,0:T(8,128)S(1)}, u32[]{:S(2)}) copy-start(f32[64,2048]{1,0:T(8,128)S(1)} %collective-permute-done) | copy-start | bytes 1572868
  155.5 12.9 %collective-permute-start.2 = (f32[64,2048]{1,0:T(8,128)S(1)}, f32[64,2048]{1,0:T(8,128)S(1)}, u32[]{:S(2)}, u32[]{:S(2)}) collective-permute-start(f32[64,2048]{1,0:T(8,128)S(1)} %collective-permute-done), channel_id=1, source_target_pairs={{0,1},{1,2},{2,3},{3,4},{4,5},{5,6},{6,7},{7,8},{8,9},{9,10},{10,1... | collective-permute-start | bytes 1572872 | tf_op jit(solution)/shard_map/ppermute | solution.py:19
  160.0 21.2 %copy-start.1 = (f32[64,2048]{1,0:T(8,128)}, f32[64,2048]{1,0:T(8,128)S(1)}, u32[]{:S(2)}) copy-start(f32[64,2048]{1,0:T(8,128)S(1)} %collective-permute-done.1) | copy-start | bytes 1572868
  160.0 19.2 %collective-permute-start.3 = (f32[64,2048]{1,0:T(8,128)S(1)}, f32[64,2048]{1,0:T(8,128)}, u32[]{:S(2)}, u32[]{:S(2)}) collective-permute-start(f32[64,2048]{1,0:T(8,128)S(1)} %collective-permute-done.1), channel_id=1, source_target_pairs={{0,15},{1,0},{2,1},{3,2},{4,3},{5,4},{6,5},{7,6},{8,7},{9,8},{10,9... | collective-permute-start | bytes 1572872 | tf_op jit(solution)/shard_map/ppermute | solution.py:24
  168.4 12.9 %collective-permute-start.4 = (f32[64,2048]{1,0:T(8,128)S(1)}, f32[64,2048]{1,0:T(8,128)S(1)}, u32[]{:S(2)}, u32[]{:S(2)}) collective-permute-start(f32[64,2048]{1,0:T(8,128)S(1)} %collective-permute-done.2), channel_id=1, source_target_pairs={{0,1},{1,2},{2,3},{3,4},{4,5},{5,6},{6,7},{7,8},{8,9},{9,10},{10,1... | collective-permute-start | bytes 1572872 | tf_op jit(solution)/shard_map/ppermute | solution.py:19
  179.3 14.6 %collective-permute-start.5 = (f32[64,2048]{1,0:T(8,128)}, f32[64,2048]{1,0:T(8,128)S(1)}, u32[]{:S(2)}, u32[]{:S(2)}) collective-permute-start(f32[64,2048]{1,0:T(8,128)} %collective-permute-done.3), channel_id=1, source_target_pairs={{0,15},{1,0},{2,1},{3,2},{4,3},{5,4},{6,5},{7,6},{8,7},{9,8},{10,9... | collective-permute-start | bytes 1572872 | tf_op jit(solution)/shard_map/ppermute | solution.py:24
  181.3 16.3 %collective-permute-start.6 = (f32[64,2048]{1,0:T(8,128)S(1)}, f32[64,2048]{1,0:T(8,128)S(1)}, u32[]{:S(2)}, u32[]{:S(2)}) collective-permute-start(f32[64,2048]{1,0:T(8,128)S(1)} %collective-permute-done.4), channel_id=1, source_target_pairs={{0,1},{1,2},{2,3},{3,4},{4,5},{5,6},{6,7},{7,8},{8,9},{9,10},{10,1... | collective-permute-start | bytes 1572872 | tf_op jit(solution)/shard_map/ppermute | solution.py:19
  193.9 8.5 %collective-permute-start.7 = (f32[64,2048]{1,0:T(8,128)S(1)}, f32[64,2048]{1,0:T(8,128)S(1)}, u32[]{:S(2)}, u32[]{:S(2)}) collective-permute-start(f32[64,2048]{1,0:T(8,128)S(1)} %collective-permute-done.5), channel_id=1, source_target_pairs={{0,15},{1,0},{2,1},{3,2},{4,3},{5,4},{6,5},{7,6},{8,7},{9,8},{10,9... | collective-permute-start | bytes 1572872 | tf_op jit(solution)/shard_map/ppermute | solution.py:24
  197.6 14.2 %collective-permute-start.8 = (f32[64,2048]{1,0:T(8,128)S(1)}, f32[64,2048]{1,0:T(8,128)S(1)}, u32[]{:S(2)}, u32[]{:S(2)}) collective-permute-start(f32[64,2048]{1,0:T(8,128)S(1)} %collective-permute-done.6), channel_id=1, source_target_pairs={{0,1},{1,2},{2,3},{3,4},{4,5},{5,6},{6,7},{7,8},{8,9},{9,10},{10,1... | collective-permute-start | bytes 1572872 | tf_op jit(solution)/shard_map/ppermute | solution.py:19
  202.4 11.8 %collective-permute-start.9 = (f32[64,2048]{1,0:T(8,128)S(1)}, f32[64,2048]{1,0:T(8,128)S(1)}, u32[]{:S(2)}, u32[]{:S(2)}) collective-permute-start(f32[64,2048]{1,0:T(8,128)S(1)} %collective-permute-done.7), channel_id=1, source_target_pairs={{0,15},{1,0},{2,1},{3,2},{4,3},{5,4},{6,5},{7,6},{8,7},{9,8},{10,9... | collective-permute-start | bytes 1572872 | tf_op jit(solution)/shard_map/ppermute | solution.py:24
  211.8 13.3 %collective-permute-start.10 = (f32[64,2048]{1,0:T(8,128)S(1)}, f32[64,2048]{1,0:T(8,128)S(1)}, u32[]{:S(2)}, u32[]{:S(2)}) collective-permute-start(f32[64,2048]{1,0:T(8,128)S(1)} %collective-permute-done.8), channel_id=1, source_target_pairs={{0,1},{1,2},{2,3},{3,4},{4,5},{5,6},{6,7},{7,8},{8,9},{9,10},{10,1... | collective-permute-start | bytes 1572872 | tf_op jit(solution)/shard_map/ppermute | solution.py:19
  214.2 12.6 %collective-permute-start.11 = (f32[64,2048]{1,0:T(8,128)S(1)}, f32[64,2048]{1,0:T(8,128)S(1)}, u32[]{:S(2)}, u32[]{:S(2)}) collective-permute-start(f32[64,2048]{1,0:T(8,128)S(1)} %collective-permute-done.9), channel_id=1, source_target_pairs={{0,15},{1,0},{2,1},{3,2},{4,3},{5,4},{6,5},{7,6},{8,7},{9,8},{10,9... | collective-permute-start | bytes 1572872 | tf_op jit(solution)/shard_map/ppermute | solution.py:24
  225.1 14.2 %collective-permute-start.12 = (f32[64,2048]{1,0:T(8,128)S(1)}, f32[64,2048]{1,0:T(8,128)S(1)}, u32[]{:S(2)}, u32[]{:S(2)}) collective-permute-start(f32[64,2048]{1,0:T(8,128)S(1)} %collective-permute-done.10), channel_id=1, source_target_pairs={{0,1},{1,2},{2,3},{3,4},{4,5},{5,6},{6,7},{7,8},{8,9},{9,10},{10,1... | collective-permute-start | bytes 1572872 | tf_op jit(solution)/shard_map/ppermute | solution.py:19
  226.8 14.3 %collective-permute-start.13 = (f32[64,2048]{1,0:T(8,128)S(1)}, f32[64,2048]{1,0:T(8,128)S(1)}, u32[]{:S(2)}, u32[]{:S(2)}) collective-permute-start(f32[64,2048]{1,0:T(8,128)S(1)} %collective-permute-done.11), channel_id=1, source_target_pairs={{0,15},{1,0},{2,1},{3,2},{4,3},{5,4},{6,5},{7,6},{8,7},{9,8},{10,9... | collective-permute-start | bytes 1572872 | tf_op jit(solution)/shard_map/ppermute | solution.py:24
  239.3 8.6 %collective-permute-start.14 = (f32[64,2048]{1,0:T(8,128)S(1)}, f32[64,2048]{1,0:T(8,128)S(1)}, u32[]{:S(2)}, u32[]{:S(2)}) collective-permute-start(f32[64,2048]{1,0:T(8,128)S(1)} %collective-permute-done.12), channel_id=1, source_target_pairs={{0,1},{1,2},{2,3},{3,4},{4,5},{5,6},{6,7},{7,8},{8,9},{9,10},{10,1... | collective-permute-start | bytes 1572872 | tf_op jit(solution)/shard_map/ppermute | solution.py:19
Sparse Core Ops, SparseCore 0:
  30.0 105.9 reduce-scatter.1
